TPU v7x, 32 devices: a whole 2x2x4 slice. The times are simulated.
32 devices in a mesh: wide: 8 (over z, x), narrow: 4 (over y, core).
Axes of the slice: x: 2, y: 2, z: 4, core: 2. Of those that a mesh axis runs over, the one named last changes fastest.
Arguments:
- embeddings: bfloat16 [16384, 768], P(('wide', 'narrow')), may hold values from -6 to 6
- coarse_ids: int32 [16384, 1], P(('wide', 'narrow')), may hold values from 0 to 7; in each aligned block of 512 rows (0 to 511, 512 to 1023, ...) at most 128 rows name the same one
- fine_ids: int32 [16384], P(('wide', 'narrow')), may hold values from 0 to 2047
- centroids: bfloat16 [16384, 768], P(('wide', 'narrow')), may hold values from -6 to 6
- candidates: int32 [128, 8], P(('wide', 'narrow')), may hold values from 0 to 63, as said below
Outputs:
- new_centroids: bfloat16 [16384, 768], P(('wide', 'narrow'))
- best_score: float32 [16384], P(('wide', 'narrow'))
Inputs may be any that keep to these rules, and one draw needn't show every extreme that they name: `candidates`: counting the 32 entries of the 4 consecutive query blocks of one device, at most 8 lie among the 8 blocks of one coarse cluster, and some coarse cluster holds exactly 8 of every device's entries.
All inputs are finite; a program needn't handle non-finite values.
Results may differ from a plain program's by a relative error of at most 0.0055.
Values may be sent and summed in bfloat16 or wider, within the bound.
A program may use at most 192 MiB of HBM per device.

v0:
```python
import jax
import jax.numpy as jnp
from jax import lax
from jax.sharding import PartitionSpec as P

QROWS = 128
CBLK = 256
K_CAND = 8


def slot_ranks(targets, count):
    table = (targets[:, None] == jnp.arange(count, dtype=jnp.int32)[None, :]).astype(jnp.int32)
    ranks = jnp.cumsum(table, axis=0) - 1
    return jnp.sum(ranks * table, axis=1)


def block_maxima(queries, table, picks):
    total, rows_n, width = queries.shape
    group = total // 8
    turns = total // group

    def one_turn(operands):
        query_part, pick_part = operands
        chosen = jnp.take(table, pick_part, axis=0)
        scores = jnp.einsum("gnd,gcd->gnc", query_part, chosen, preferred_element_type=jnp.float32)
        return jnp.max(scores, axis=2)

    result = lax.map(
        one_turn, (queries.reshape(turns, group, rows_n, width), picks.reshape(turns, group))
    )
    return result.reshape(total, rows_n) * width ** (-0.5)


def local(embeddings, coarse_ids, fine_ids, centroids, candidates):
    wide_count = lax.axis_size("wide")
    narrow_count = lax.axis_size("narrow")
    emb_rows, width = embeddings.shape
    cent_rows = centroids.shape[0]
    group_cents = cent_rows * narrow_count
    row_cap = (2 * emb_rows + wide_count - 1) // wide_count
    targets = coarse_ids[:, 0]
    row_pos = targets * row_cap + slot_ranks(targets, wide_count)
    send_rows = jnp.zeros((wide_count * row_cap, width), jnp.bfloat16).at[row_pos].set(embeddings)
    send_fine = jnp.full((wide_count * row_cap,), -1, jnp.int32).at[row_pos].set(fine_ids)
    recv_rows, recv_fine = (
        lax.all_to_all(
            send_rows.reshape(wide_count, row_cap, width),
            "wide",
            split_axis=0,
            concat_axis=0,
            tiled=True,
        ),
        lax.all_to_all(
            send_fine.reshape(wide_count, row_cap), "wide", split_axis=0, concat_axis=0, tiled=True
        ),
    )
    flat_rows = recv_rows.reshape(-1, width)
    flat_fine = recv_fine.reshape(-1)
    columns = jnp.arange(lax.axis_size("narrow") * cent_rows, dtype=jnp.int32)
    one_hot = (flat_fine[:, None] == columns[None, :]).astype(jnp.bfloat16)
    sums = lax.psum_scatter(
        lax.dot_general(
            one_hot, flat_rows, (((0,), (0,)), ((), ())), preferred_element_type=jnp.float32
        ).astype(jnp.bfloat16),
        "narrow",
        scatter_dimension=0,
        tiled=True,
    ).astype(jnp.float32)
    mixed = centroids.astype(jnp.float32) + sums
    scale_row = lax.rsqrt(jnp.mean(mixed * mixed, axis=1, keepdims=True) + 1e-06)
    new_centroids = (mixed * scale_row).astype(jnp.bfloat16)
    gathered = lax.all_gather(new_centroids, "narrow", axis=0, tiled=True)
    block_count = group_cents // CBLK
    block_table = gathered.reshape(block_count, CBLK, width)
    query_count = emb_rows // QROWS
    requests = query_count * K_CAND
    slot_cap = (2 * requests + wide_count - 1) // wide_count
    slot_total = wide_count * slot_cap
    wanted = candidates.reshape(-1)
    owner_group = wanted // block_count
    local_block = wanted - owner_group * block_count
    req_pos = owner_group * slot_cap + slot_ranks(owner_group, wide_count)
    req_query = jnp.arange(requests, dtype=jnp.int32) // K_CAND
    slot_query = jnp.zeros((slot_total,), jnp.int32).at[req_pos].set(req_query)
    slot_live = jnp.zeros((slot_total,), jnp.bool_).at[req_pos].set(True)
    slot_block = jnp.full((slot_total,), -1, jnp.int32).at[req_pos].set(local_block)
    query_blocks = embeddings.reshape(query_count, QROWS, width)
    send_queries = jnp.where(
        slot_live[:, None, None],
        jnp.take(query_blocks, slot_query, axis=0),
        jnp.zeros((), jnp.bfloat16),
    )
    ids_in = lax.all_to_all(
        slot_block.reshape(wide_count, slot_cap), "wide", split_axis=0, concat_axis=0, tiled=True
    )
    picks = jnp.clip(ids_in.reshape(-1), 0, block_count - 1)
    outgoing = jnp.take(block_table, picks, axis=0).reshape(wide_count, slot_cap, CBLK, width)
    fetched = lax.all_to_all(outgoing, "wide", split_axis=0, concat_axis=0, tiled=True)
    values = block_maxima(
        send_queries,
        fetched.reshape(slot_total, CBLK, width),
        jnp.arange(slot_total, dtype=jnp.int32),
    )
    per_request = jnp.take(values, req_pos, axis=0)
    best_score = jnp.max(per_request.reshape(query_count, K_CAND, QROWS), axis=1).reshape(emb_rows)
    return (new_centroids, best_score)


def solution(mesh):
    return jax.shard_map(
        local,
        mesh=mesh,
        in_specs=(
            P(("wide", "narrow"), None),
            P(("wide", "narrow"), None),
            P(("wide", "narrow")),
            P(("wide", "narrow"), None),
            P(("wide", "narrow"), None),
        ),
        out_specs=(P(("wide", "narrow"), None), P(("wide", "narrow"))),
        check_vma=False,
    )
```

profile of v0, /device:TPU:0, one launch (start us, length us, event | category | flops | bytes accessed | tf_op | source)
XLA Modules:
  0.0 827.4 jit_solution(12097914941548033054)
XLA Ops:
  10.7 3.2 scatter_custom_fusion
  13.9 7.3 all-to-all-start
  21.2 3.6 scatter_custom_fusion.1
  24.7 2.8 all-to-all-done
  27.5 39.5 %all_to_all.28 = bf16[8,128,768]{2,1,0:T(8,128)(2,1)S(1)} all-to-all(bf16[8,128,768]{2,1,0:T(8,128)(2,1)S(1)} %bitcast.70), channel_id=1, replica_groups=mesh['wide'=8,'narrow'=4] {'wide'}, dimensions={0} | all-to-all | bytes 3145728 | tf_op jit(solution)/shard_map/all_to_all | solution.py:46
  67.0 5.9 fusion.16
  73.0 37.0 %reduce-scatter.2.cloned.1.call-done = bf16[512,768]{1,0:T(8,128)(2,1)} async-done(((bf16[2048,768]{1,0:T(8,128)(2,1)}), bf16[512,768]{1,0:T(8,128)(2,1)}) %reduce-scatter.2.cloned.1.call-update) | async-done | bytes 786448 | tf_op jit(solution)/shard_map/reduce_scatter | solution.py:61
  115.1 11.8 %all_to_all.29 = s32[8,1,8]{2,1,0:T(1,128)S(1)} all-to-all(s32[8,1,8]{2,1,0:T(1,128)S(1)} %bitcast.76), channel_id=1, replica_groups=mesh['wide'=8,'narrow'=4] {'wide'}, dimensions={0} | all-to-all | bytes 512 | tf_op jit(solution)/shard_map/all_to_all | solution.py:93
  127.0 15.5 %all-gather.2.cloned.1.call-done = bf16[2048,768]{1,0:T(8,128)(2,1)} async-done(((bf16[512,768]{1,0:T(8,128)(2,1)}), bf16[2048,768]{1,0:T(8,128)(2,1)}) %all-gather.2.cloned.1.call-update) | async-done | bytes 3145744 | tf_op jit(solution)/shard_map/all_gather | solution.py:72
  142.5 12.1 %gather_fusion.2 = bf16[64,256,768]{2,1,0:T(8,128)(2,1)} fusion(bf16[8,256,768]{2,1,0:T(8,128)(2,1)} %bitcast.66, s32[1024]{0:T(1024)S(1)} %pad_clamp_fusion.2), kind=kCustom, calls=%fused_computation.2 | custom fusion | bytes 50331904 | tf_op jit(solution)/shard_map/jit(_take)/gather | solution.py:97
  154.6 21.3 %broadcast_select_fusion = bf16[8,8,256,768]{3,2,1,0:T(8,128)(2,1)} fusion(bf16[8,8,256,768]{3,2,1,0:T(8,128)(2,1)} %bitcast.68, pred[8,8]{1,0:T(8,128)(4,1)S(1)} %compare_and_fusion.1), kind=kLoop, calls=%fused_computation.25 | loop fusion | flops 12582912 | bytes 50331712 | tf_op jit(solution)/shard_map/jit(_take)/select_n | solution.py:97
  175.9 6.6 all-to-all-start.3
  184.3 7.0 gather_fusion.1
  191.4 11.1 %select_select_fusion = bf16[8,8,128,768]{3,2,1,0:T(8,128)(2,1)} fusion(bf16[8,8,128,768]{3,2,1,0:T(8,128)(2,1)} %bitcast.69, pred[8,8]{1,0:T(8,128)(4,1)S(1)} %broadcast_in_dim.109, pred[8,8]{1,0:T(8,128)(4,1)S(1)} %broadcast_in_dim.106), kind=kLoop, calls=%fused_computation.26 | loop fusion | flops 12582912 | bytes 25165952 | tf_op jit(solution)/shard_map/jit(_where)/select_n | solution.py:88
  202.5 523.1 %all-to-all-done.3 = bf16[8,8,256,768]{3,2,1,0:T(8,128)(2,1)} async-done(((bf16[8,8,256,768]{3,2,1,0:T(8,128)(2,1)}), bf16[8,8,256,768]{3,2,1,0:T(8,128)(2,1)}, u32[]{:S(2)}, u32[]{:S(2)}) %all-to-all-start.3) | async-done | bytes 25165856 | tf_op jit(solution)/shard_map/all_to_all | solution.py:98
  725.6 93.7 %while.10 = (s32[]{:T(128)}, f32[8,8,128]{2,1,0:T(8,128)S(1)}, bf16[8,8,128,768]{3,2,1,0:T(8,128)(2,1)}, s32[8,8]{1,0:T(8,128)S(1)}, bf16[64,256,768]{2,1,0:T(8,128)(2,1)}, /*index=5*/s32[]{:T(128)}) while((s32[]{:T(128)}, f32[8,8,128]{2,1,0:T(8,128)S(1)}, bf16[8,8,128,768]{3,2,1,0:T(8,128)(2,1)}, s32[8,8]{1,0:T(8,128)S(1)}, ...), condition=%wide.region_14.15_spmd, body=%wide.region_12.14_spmd.sunk | while | flops 404488256 | bytes 11027201 | solution.py:28
  725.7 8.9 %gather_fusion = bf16[8,256,768]{2,1,0:T(8,128)(2,1)S(1)} fusion(bf16[64,256,768]{2,1,0:T(8,128)(2,1)} %get-tuple-element.89, s32[1024]{0:T(1024)S(1)} %pad_clamp_fusion.5), kind=kCustom, calls=%fused_computation.clone.1 | custom fusion | bytes 6291488 | tf_op jit(solution)/shard_map/while/body/eval_jaxpr/jit(_take)/gather | solution.py:24
  734.6 2.7 fusion.45
  737.4 8.9 %gather_fusion = bf16[8,256,768]{2,1,0:T(8,128)(2,1)S(1)} fusion(bf16[64,256,768]{2,1,0:T(8,128)(2,1)} %get-tuple-element.89, s32[1024]{0:T(1024)S(1)} %pad_clamp_fusion.5), kind=kCustom, calls=%fused_computation.clone.1 | custom fusion | bytes 6291488 | tf_op jit(solution)/shard_map/while/body/eval_jaxpr/jit(_take)/gather | solution.py:24
  746.3 2.7 fusion.45
  749.1 8.9 %gather_fusion = bf16[8,256,768]{2,1,0:T(8,128)(2,1)S(1)} fusion(bf16[64,256,768]{2,1,0:T(8,128)(2,1)} %get-tuple-element.89, s32[1024]{0:T(1024)S(1)} %pad_clamp_fusion.5), kind=kCustom, calls=%fused_computation.clone.1 | custom fusion | bytes 6291488 | tf_op jit(solution)/shard_map/while/body/eval_jaxpr/jit(_take)/gather | solution.py:24
  758.0 2.7 fusion.45
  760.8 8.9 %gather_fusion = bf16[8,256,768]{2,1,0:T(8,128)(2,1)S(1)} fusion(bf16[64,256,768]{2,1,0:T(8,128)(2,1)} %get-tuple-element.89, s32[1024]{0:T(1024)S(1)} %pad_clamp_fusion.5), kind=kCustom, calls=%fused_computation.clone.1 | custom fusion | bytes 6291488 | tf_op jit(solution)/shard_map/while/body/eval_jaxpr/jit(_take)/gather | solution.py:24
  769.7 2.7 fusion.45
  772.5 8.9 %gather_fusion = bf16[8,256,768]{2,1,0:T(8,128)(2,1)S(1)} fusion(bf16[64,256,768]{2,1,0:T(8,128)(2,1)} %get-tuple-element.89, s32[1024]{0:T(1024)S(1)} %pad_clamp_fusion.5), kind=kCustom, calls=%fused_computation.clone.1 | custom fusion | bytes 6291488 | tf_op jit(solution)/shard_map/while/body/eval_jaxpr/jit(_take)/gather | solution.py:24
  781.5 2.7 fusion.45
  784.2 8.9 %gather_fusion = bf16[8,256,768]{2,1,0:T(8,128)(2,1)S(1)} fusion(bf16[64,256,768]{2,1,0:T(8,128)(2,1)} %get-tuple-element.89, s32[1024]{0:T(1024)S(1)} %pad_clamp_fusion.5), kind=kCustom, calls=%fused_computation.clone.1 | custom fusion | bytes 6291488 | tf_op jit(solution)/shard_map/while/body/eval_jaxpr/jit(_take)/gather | solution.py:24
  793.2 2.7 fusion.45
  795.9 8.9 %gather_fusion = bf16[8,256,768]{2,1,0:T(8,128)(2,1)S(1)} fusion(bf16[64,256,768]{2,1,0:T(8,128)(2,1)} %get-tuple-element.89, s32[1024]{0:T(1024)S(1)} %pad_clamp_fusion.5), kind=kCustom, calls=%fused_computation.clone.1 | custom fusion | bytes 6291488 | tf_op jit(solution)/shard_map/while/body/eval_jaxpr/jit(_take)/gather | solution.py:24
  804.9 2.7 fusion.45
  807.7 8.9 %gather_fusion = bf16[8,256,768]{2,1,0:T(8,128)(2,1)S(1)} fusion(bf16[64,256,768]{2,1,0:T(8,128)(2,1)} %get-tuple-element.89, s32[1024]{0:T(1024)S(1)} %pad_clamp_fusion.5), kind=kCustom, calls=%fused_computation.clone.1 | custom fusion | bytes 6291488 | tf_op jit(solution)/shard_map/while/body/eval_jaxpr/jit(_take)/gather | solution.py:24
  816.6 2.7 fusion.45
  (83 shorter events, 12.2 us)
Async XLA Ops:
  13.9 13.6 %all-to-all-start = ((s32[8,1,128]{2,1,0:T(1,128)}), s32[8,1,128]{2,1,0:T(1,128)S(1)}, u32[]{:S(2)}, u32[]{:S(2)}) async-start(s32[8,1,128]{2,1,0:T(1,128)} %bitcast.11), calls=%async_computation | async-start | bytes 8192 | tf_op jit(solution)/shard_map/all_to_all | solution.py:53
  21.1 88.9 %reduce-scatter.2.cloned.1.call-start = ((), (), s32[]{:S(2)}) async-start(), calls=%async_computation.5 | async-start | bytes 3932160 | tf_op jit(solution)/shard_map/reduce_scatter | solution.py:61
  72.9 37.1 %copy-start.1 = (bf16[512,768]{1,0:T(8,128)(2,1)S(1)}, bf16[512,768]{1,0:T(8,128)(2,1)}, u32[]{:S(2)}) copy-start(bf16[512,768]{1,0:T(8,128)(2,1)} %param.10) | copy-start | bytes 2359300
  72.9 40.9 %copy-start.2 = (s32[4,8]{1,0:T(4,128)S(1)}, s32[4,8]{1,0:T(4,128)}, u32[]{:S(2)}) copy-start(s32[4,8]{1,0:T(4,128)} %param.11) | copy-start | bytes 388
  72.9 69.5 %all-gather.2.cloned.1.call-start = ((), (), s32[]{:S(2)}) async-start(), calls=%async_computation.6 | async-start | bytes 3932160 | tf_op jit(solution)/shard_map/all_gather | solution.py:72
  175.9 8.4 %copy-start = (bf16[512,768]{1,0:T(8,128)(2,1)S(1)}, bf16[512,768]{1,0:T(8,128)(2,1)}, u32[]{:S(2)}) copy-start(bf16[512,768]{1,0:T(8,128)(2,1)} %param.7) | copy-start | bytes 2359300
  175.9 549.8 %all-to-all-start.3 = ((bf16[8,8,256,768]{3,2,1,0:T(8,128)(2,1)}), bf16[8,8,256,768]{3,2,1,0:T(8,128)(2,1)}, u32[]{:S(2)}, u32[]{:S(2)}) async-start(bf16[8,8,256,768]{3,2,1,0:T(8,128)(2,1)} %broadcast_select_fusion), calls=%async_computation.4 | async-start | bytes 50331648 | tf_op jit(solution)/shard_map/all_to_all | solution.py:98
Sparse Core Ops, SparseCore 0:
  73.1 36.9 reduce-scatter.1
  113.9 28.5 all-gather.1
where the time goes:
time: 829 us; the launch traced here: 827 us
  waiting for transfers between devices  579 us (70%)
  local copies, waits for them, and re-layouts  101 us (12%)
  blocking collectives  51.2 us (6%)
  other arithmetic  40.8 us (5%)
  matrix products  27.6 us (3%)
  between operations  14.2 us (2%)
  starting transfers between devices  13.9 us (2%)
    all_to_all x1, waiting for transfers between devices, local(): lax.all_to_all(outgoing, 'wide', split_axis=0, concat_axis=0, tiled=True)  523 us
    gather x8, local copies, waits for them, and re-layouts, one_turn(): chosen = jnp.take(table, pick_part, axis=0)  71.2 us
    all_to_all x1, blocking collectives, local(): lax.all_to_all(send_rows.reshape(wide_count, row_cap, width), 'wide', spl...  39.5 us
    reduce_scatter x1, waiting for transfers between devices, local(): lax.psum_scatter(lax.dot_general(one_hot, flat_rows, (((0,), (0,)), ((),...  37 us
    dot_general x8, matrix products, one_turn(): jnp.einsum('gnd,gcd->gnc', query_part, chosen, preferred_element_type=jnp...  21.7 us
    select_n x2, other arithmetic, local(): jnp.take(block_table, picks, axis=0)  21.3 us
  transfers between devices with their start and end apart: 4, of which 4 were waited for; matrix products, arithmetic and copies ran while one was open for 3% of the time, Pallas kernels for 0%

commit v1 on v0

--- a/solution.py
+++ b/solution.py
@@ -6,6 +6,17 @@
 QROWS = 128
 CBLK = 256
 K_CAND = 8
+
+
+def teams_take(local_values, d0, x_in):
+    upper, val2 = (local_values.shape[:d0], local_values.shape[d0 + 1 :])
+    return jnp.moveaxis(local_values.reshape(*upper, x_in, -1, *val2), d0, 0)
+
+
+def _store_node(inner_x, pos_dim):
+    main = list(inner_x.shape[1:])
+    main[pos_dim] *= inner_x.shape[0]
+    return jnp.moveaxis(inner_x, 0, pos_dim).reshape(main)
 
 
 def slot_ranks(targets, count):
@@ -95,7 +106,20 @@
     )
     picks = jnp.clip(ids_in.reshape(-1), 0, block_count - 1)
     outgoing = jnp.take(block_table, picks, axis=0).reshape(wide_count, slot_cap, CBLK, width)
-    fetched = lax.all_to_all(outgoing, "wide", split_axis=0, concat_axis=0, tiled=True)
+    passed = lax.axis_size("wide")
+    answer, inter = (passed, lax.axis_index("wide"))
+    new = teams_take(outgoing, 0, answer)
+    series = [new[inter]]
+    idx = 1
+    while idx < answer:
+        base_arr = new[(inter + idx) % answer]
+        oldest = lax.ppermute(
+            base_arr, "wide", [(nth, (nth + idx) % answer) for nth in range(answer)]
+        )
+        series.append(oldest)
+        idx += 1
+    new = jnp.stack(series, axis=0)[(inter - jnp.arange(answer)) % answer]
+    fetched = _store_node(new, 0)
     values = block_maxima(
         send_queries,
         fetched.reshape(slot_total, CBLK, width),

time: 829 us -> 895 us (1.080)
  the two profiles are of different devices: /device:TPU:0 before, /device:TPU:26 now
where the time goes in v1:
time: 895 us; the launch traced here: 894 us
  waiting for transfers between devices  563 us (63%)
  local copies, waits for them, and re-layouts  168 us (19%)
  other arithmetic  61.8 us (7%)
  blocking collectives  39.8 us (4%)
  matrix products  27.6 us (3%)
  starting transfers between devices  19.1 us (2%)
  between operations  14.2 us (2%)
    ppermute x7, waiting for transfers between devices, local(): lax.ppermute(base_arr, 'wide', [(nth, (nth + idx) % answer) for nth in ra...  503 us
    gather x8, local copies, waits for them, and re-layouts, one_turn(): chosen = jnp.take(table, pick_part, axis=0)  71.3 us
    all_to_all x1, blocking collectives, local(): lax.all_to_all(send_rows.reshape(wide_count, row_cap, width), 'wide', spl...  39.8 us
    reduce_scatter x1, waiting for transfers between devices, local(): lax.psum_scatter(lax.dot_general(one_hot, flat_rows, (((0,), (0,)), ((),...  39 us
    gather x3, local copies, waits for them, and re-layouts, local(): new = jnp.stack(series, axis=0)[(inter - jnp.arange(answer)) % answer]  32.9 us
    dot_general x8, matrix products, one_turn(): jnp.einsum('gnd,gcd->gnc', query_part, chosen, preferred_element_type=jnp...  21.7 us
    select_n x2, other arithmetic, local(): jnp.take(block_table, picks, axis=0)  21.3 us
    unnamed x1, other arithmetic  20.4 us
  transfers between devices with their start and end apart: 11, of which 7 were waited for; matrix products, arithmetic and copies ran while one was open for 4% of the time, Pallas kernels for 0%

profile of v1, /device:TPU:26, one launch (start us, length us, event | category | flops | bytes accessed | tf_op | source)
XLA Modules:
  0.0 893.9 jit_solution(7042562999426527852)
XLA Ops:
  10.7 3.2 scatter_custom_fusion
  13.9 6.0 all-to-all-start
  19.9 3.6 scatter_custom_fusion.1
  23.4 39.8 %all_to_all.23 = bf16[8,128,768]{2,1,0:T(8,128)(2,1)S(1)} all-to-all(bf16[8,128,768]{2,1,0:T(8,128)(2,1)S(1)} %bitcast.109), channel_id=1, replica_groups=mesh['wide'=8,'narrow'=4] {'wide'}, dimensions={0} | all-to-all | bytes 3145728 | tf_op jit(solution)/shard_map/all_to_all | solution.py:57
  63.3 5.9 fusion.16
  69.3 39.0 %reduce-scatter.2.cloned.1.call-done = bf16[512,768]{1,0:T(8,128)(2,1)} async-done(((bf16[2048,768]{1,0:T(8,128)(2,1)}), bf16[512,768]{1,0:T(8,128)(2,1)}) %reduce-scatter.2.cloned.1.call-update) | async-done | bytes 786448 | tf_op jit(solution)/shard_map/reduce_scatter | solution.py:72
  113.9 6.0 all-to-all-start.2
  122.4 18.4 %all-gather.2.cloned.1.call-done = bf16[2048,768]{1,0:T(8,128)(2,1)} async-done(((bf16[512,768]{1,0:T(8,128)(2,1)}), bf16[2048,768]{1,0:T(8,128)(2,1)}) %all-gather.2.cloned.1.call-update) | async-done | bytes 3145744 | tf_op jit(solution)/shard_map/all_gather | solution.py:83
  140.7 12.3 %gather_fusion.2 = bf16[64,256,768]{2,1,0:T(8,128)(2,1)} fusion(bf16[8,256,768]{2,1,0:T(8,128)(2,1)} %bitcast.102, s32[1024]{0:T(1024)S(1)} %pad_clamp_fusion.3), kind=kCustom, calls=%fused_computation.2 | custom fusion | bytes 50331904 | tf_op jit(solution)/shard_map/jit(_take)/gather | solution.py:108
  153.0 21.3 %broadcast_select_fusion = bf16[8,1,8,256,768]{4,3,2,0,1:T(8,128)(2,1)} fusion(bf16[8,1,8,256,768]{4,3,2,0,1:T(8,128)(2,1)} %bitcast.104, pred[8,8]{1,0:T(8,128)(4,1)S(1)} %compare_and_fusion.1), kind=kLoop, calls=%fused_computation.28 | loop fusion | flops 12582912 | bytes 50331712 | tf_op jit(solution)/shard_map/jit(_take)/select_n | solution.py:108
  174.3 17.2 %dynamic-slice_bitcast_fusion = (bf16[1,8,256,768]{3,2,1,0:T(8,128)(2,1)}, bf16[1,8,256,768]{3,2,1,0:T(8,128)(2,1)}, bf16[1,8,256,768]{3,2,1,0:T(8,128)(2,1)}, b...) fusion(bf16[8,1,8,256,768]{4,3,2,0,1:T(8,128)(2,1)} %broadcast_, ...), kind=kLoop, calls=%fused_computation.43 | loop fusion | bytes 50331680 | tf_op jit(solution)/shard_map/squeeze | solution.py:115
  200.0 7.2 gather_fusion.1
  207.2 55.0 %collective-permute-done = bf16[1,8,256,768]{3,2,1,0:T(8,128)(2,1)} collective-permute-done((bf16[1,8,256,768]{3,2,1,0:T(8,128)(2,1)}, bf16[1,8,256,768]{3,2,1,0:T(8,128)(2,1)}, u32[]{:S(2)}, u32[]{:S(2)}) %collective-permute-start) | collective-permute-done | bytes 3145760 | tf_op jit(solution)/shard_map/ppermute | solution.py:116
  262.7 67.1 %collective-permute-done.1 = bf16[1,8,256,768]{3,2,1,0:T(8,128)(2,1)} collective-permute-done((bf16[1,8,256,768]{3,2,1,0:T(8,128)(2,1)}, bf16[1,8,256,768]{3,2,1,0:T(8,128)(2,1)}, u32[]{:S(2)}, u32[]{:S(2)}) %collective-permute-start.1) | collective-permute-done | bytes 3145760 | tf_op jit(solution)/shard_map/ppermute | solution.py:116
  329.8 11.7 %select_select_fusion = bf16[8,8,128,768]{3,2,1,0:T(8,128)(2,1)} fusion(bf16[8,8,128,768]{3,2,1,0:T(8,128)(2,1)} %bitcast.106, pred[8,8]{1,0:T(8,128)(4,1)S(1)} %broadcast_in_dim.110, pred[8,8]{1,0:T(8,128)(4,1)S(1)} %broadcast_in_dim.107), kind=kLoop, calls=%fused_computation.31 | loop fusion | flops 12582912 | bytes 25165952 | tf_op jit(solution)/shard_map/jit(_where)/select_n | solution.py:99
  341.5 4.9 copy-done.1
  350.6 45.2 %collective-permute-done.2 = bf16[1,8,256,768]{3,2,1,0:T(8,128)(2,1)} collective-permute-done((bf16[1,8,256,768]{3,2,1,0:T(8,128)(2,1)}, bf16[1,8,256,768]{3,2,1,0:T(8,128)(2,1)}, u32[]{:S(2)}, u32[]{:S(2)}) %collective-permute-start.2) | collective-permute-done | bytes 3145760 | tf_op jit(solution)/shard_map/ppermute | solution.py:116
  397.9 336.1 %collective-permute-done.3 = bf16[1,8,256,768]{3,2,1,0:T(8,128)(2,1)} collective-permute-done((bf16[1,8,256,768]{3,2,1,0:T(8,128)(2,1)}, bf16[1,8,256,768]{3,2,1,0:T(8,128)(2,1)}, u32[]{:S(2)}, u32[]{:S(2)}) %collective-permute-start.3) | collective-permute-done | bytes 3145760 | tf_op jit(solution)/shard_map/ppermute | solution.py:116
  738.8 10.2 %slice_bitcast_fusion.1 = (bf16[8,8,256,384]{3,2,1,0:T(8,128)(2,1)}, bf16[8,8,256,384]{3,2,1,0:T(8,128)(2,1)}) fusion(bf16[8,1,8,256,768]{4,3,2,0,1:T(8,128)(2,1)S(1)} %bitcast_dynamic-update-slice_fusion.1), kind=kLoop, calls=%fused_computation.30 | loop fusion | bytes 50331648 | tf_op jit(solution)/shard_map/gather | solution.py:121
  748.9 11.3 %gather_fusion.4 = bf16[8,8,256,384]{3,2,1,0:T(8,128)(2,1)} fusion(bf16[8,8,256,384]{3,2,1,0:T(8,128)(2,1)} %get-tuple-element.42, s32[1024]{0:T(1024)S(1)} %pad_clamp_fusion.2), kind=kCustom, calls=%fused_computation.4 | custom fusion | bytes 25165856 | tf_op jit(solution)/shard_map/gather | solution.py:121
  760.3 11.4 %gather_fusion.5 = bf16[8,8,256,384]{3,2,1,0:T(8,128)(2,1)} fusion(bf16[8,8,256,384]{3,2,1,0:T(8,128)(2,1)} %get-tuple-element.43, s32[1024]{0:T(1024)S(1)} %pad_clamp_fusion.2), kind=kCustom, calls=%fused_computation.5 | custom fusion | bytes 25165856 | tf_op jit(solution)/shard_map/gather | solution.py:121
  771.6 20.4 %pad_maximum_fusion = bf16[8,1,8,256,768]{4,3,2,0,1:T(8,128)(2,1)} fusion(bf16[8,1,8,256,384]{4,3,2,0,1:T(8,128)(2,1)} %bitcast.108, bf16[8,1,8,256,384]{4,3,2,0,1:T(8,128)(2,1)} %bitcast.107), kind=kLoop, calls=%fused_computation.27 | loop fusion | flops 50331648 | bytes 50331648
  792.1 93.7 %while.10 = (s32[]{:T(128)}, f32[8,8,128]{2,1,0:T(8,128)S(1)}, bf16[8,8,128,768]{3,2,1,0:T(8,128)(2,1)}, s32[8,8]{1,0:T(8,128)S(1)}, bf16[64,256,768]{2,1,0:T(8,128)(2,1)}, /*index=5*/s32[]{:T(128)}) while((s32[]{:T(128)}, f32[8,8,128]{2,1,0:T(8,128)S(1)}, bf16[8,8,128,768]{3,2,1,0:T(8,128)(2,1)}, s32[8,8]{1,0:T(8,128)S(1)}, ...), condition=%wide.region_14.15_spmd, body=%wide.region_12.14_spmd.sunk | while | flops 404488256 | bytes 11027201 | solution.py:39
  792.1 8.9 gather_fusion
  801.0 2.7 fusion.47
  803.8 8.9 gather_fusion
  815.5 8.9 gather_fusion
  827.2 8.9 gather_fusion
  838.9 8.9 gather_fusion
  850.7 8.9 gather_fusion
  862.4 8.9 gather_fusion
  874.1 8.9 gather_fusion
  (111 shorter events, 52.1 us)
Async XLA Ops:
  13.9 9.6 %all-to-all-start = ((s32[8,1,128]{2,1,0:T(1,128)}), s32[8,1,128]{2,1,0:T(1,128)S(1)}, u32[]{:S(2)}, u32[]{:S(2)}) async-start(s32[8,1,128]{2,1,0:T(1,128)} %bitcast.11), calls=%async_computation | async-start | bytes 8192 | tf_op jit(solution)/shard_map/all_to_all | solution.py:64
  19.9 88.4 %reduce-scatter.2.cloned.1.call-start = ((), (), s32[]{:S(2)}) async-start(), calls=%async_computation.4 | async-start | bytes 3932160 | tf_op jit(solution)/shard_map/reduce_scatter | solution.py:72
  63.3 45.0 %copy-start.2 = (bf16[512,768]{1,0:T(8,128)(2,1)S(1)}, bf16[512,768]{1,0:T(8,128)(2,1)}, u32[]{:S(2)}) copy-start(bf16[512,768]{1,0:T(8,128)(2,1)} %param.10) | copy-start | bytes 2359300
  63.3 48.8 %copy-start.3 = (s32[4,8]{1,0:T(4,128)S(1)}, s32[4,8]{1,0:T(4,128)}, u32[]{:S(2)}) copy-start(s32[4,8]{1,0:T(4,128)} %param.11) | copy-start | bytes 388
  69.2 71.5 %all-gather.2.cloned.1.call-start = ((), (), s32[]{:S(2)}) async-start(), calls=%async_computation.5 | async-start | bytes 3932160 | tf_op jit(solution)/shard_map/all_gather | solution.py:83
  113.9 8.3 all-to-all-start.2
  174.3 25.6 %copy-start = (bf16[512,768]{1,0:T(8,128)(2,1)S(1)}, bf16[512,768]{1,0:T(8,128)(2,1)}, u32[]{:S(2)}) copy-start(bf16[512,768]{1,0:T(8,128)(2,1)} %param.7) | copy-start | bytes 2359300
  191.5 70.7 %collective-permute-start = (bf16[1,8,256,768]{3,2,1,0:T(8,128)(2,1)}, bf16[1,8,256,768]{3,2,1,0:T(8,128)(2,1)}, u32[]{:S(2)}, u32[]{:S(2)}) collective-permute-start(bf16[1,8,256,768]{3,2,1,0:T(8,128)(2,1)} %get-tuple-element.50), channel_id=1, source_target_pairs={{0,4},{4,8},{8,12},{12,16},{16,20},{20,24},{24,28},{28,0},{1,5},{5... | collective-permute-start | bytes 9437192 | tf_op jit(solution)/shard_map/ppermute | solution.py:116
  192.1 137.7 %collective-permute-start.1 = (bf16[1,8,256,768]{3,2,1,0:T(8,128)(2,1)}, bf16[1,8,256,768]{3,2,1,0:T(8,128)(2,1)}, u32[]{:S(2)}, u32[]{:S(2)}) collective-permute-start(bf16[1,8,256,768]{3,2,1,0:T(8,128)(2,1)} %get-tuple-element.49), channel_id=1, source_target_pairs={{0,8},{4,12},{8,16},{12,20},{16,24},{20,28},{24,0},{28,4},{1,9},{5... | collective-permute-start | bytes 9437192 | tf_op jit(solution)/shard_map/ppermute | solution.py:116
  193.7 202.1 %collective-permute-start.2 = (bf16[1,8,256,768]{3,2,1,0:T(8,128)(2,1)}, bf16[1,8,256,768]{3,2,1,0:T(8,128)(2,1)}, u32[]{:S(2)}, u32[]{:S(2)}) collective-permute-start(bf16[1,8,256,768]{3,2,1,0:T(8,128)(2,1)} %get-tuple-element.48), channel_id=1, source_target_pairs={{0,12},{4,16},{8,20},{12,24},{16,28},{20,0},{24,4},{28,8},{1,13},{... | collective-permute-start | bytes 9437192 | tf_op jit(solution)/shard_map/ppermute | solution.py:116
  195.7 538.3 %collective-permute-start.3 = (bf16[1,8,256,768]{3,2,1,0:T(8,128)(2,1)}, bf16[1,8,256,768]{3,2,1,0:T(8,128)(2,1)}, u32[]{:S(2)}, u32[]{:S(2)}) collective-permute-start(bf16[1,8,256,768]{3,2,1,0:T(8,128)(2,1)} %get-tuple-element.47), channel_id=1, source_target_pairs={{0,16},{4,20},{8,24},{12,28},{16,0},{20,4},{24,8},{28,12},{1,17},{... | collective-permute-start | bytes 9437192 | tf_op jit(solution)/shard_map/ppermute | solution.py:116
  197.3 538.8 %collective-permute-start.4 = (bf16[1,8,256,768]{3,2,1,0:T(8,128)(2,1)}, bf16[1,8,256,768]{3,2,1,0:T(8,128)(2,1)}, u32[]{:S(2)}, u32[]{:S(2)}) collective-permute-start(bf16[1,8,256,768]{3,2,1,0:T(8,128)(2,1)} %get-tuple-element.46), channel_id=1, source_target_pairs={{0,20},{4,24},{8,28},{12,0},{16,4},{20,8},{24,12},{28,16},{1,21},{... | collective-permute-start | bytes 9437192 | tf_op jit(solution)/shard_map/ppermute | solution.py:116
  262.2 476.1 %collective-permute-start.5 = (bf16[1,8,256,768]{3,2,1,0:T(8,128)(2,1)}, bf16[1,8,256,768]{3,2,1,0:T(8,128)(2,1)S(1)}, u32[]{:S(2)}, u32[]{:S(2)}) collective-permute-start(bf16[1,8,256,768]{3,2,1,0:T(8,128)(2,1)} %get-tuple-element.45), channel_id=1, source_target_pairs={{0,24},{4,28},{8,0},{12,4},{16,8},{20,12},{24,16},{28,20},{1,25},{... | collective-permute-start | bytes 9437192 | tf_op jit(solution)/shard_map/ppermute | solution.py:116
  329.8 408.7 %collective-permute-start.6 = (bf16[1,8,256,768]{3,2,1,0:T(8,128)(2,1)}, bf16[1,8,256,768]{3,2,1,0:T(8,128)(2,1)S(1)}, u32[]{:S(2)}, u32[]{:S(2)}) collective-permute-start(bf16[1,8,256,768]{3,2,1,0:T(8,128)(2,1)} %get-tuple-element.44), channel_id=1, source_target_pairs={{0,28},{4,0},{8,4},{12,8},{16,12},{20,16},{24,20},{28,24},{1,29},{... | collective-permute-start | bytes 9437192 | tf_op jit(solution)/shard_map/ppermute | solution.py:116
  329.8 16.6 %copy-start.1 = (bf16[8,1,8,256,768]{4,3,2,0,1:T(8,128)(2,1)S(1)}, bf16[8,1,8,256,768]{4,3,2,0,1:T(8,128)(2,1)}, u32[]{:S(2)}) copy-start(bf16[8,1,8,256,768]{4,3,2,0,1:T(8,128)(2,1)} %get-tuple-element.51) | copy-start | bytes 75497472
Sparse Core Ops, SparseCore 0:
  69.3 38.8 reduce-scatter.1
  112.2 28.5 all-gather.1
